TPU v7x, 256 devices: a whole 4x4x8 slice. The times are simulated.
256 devices in a mesh: tm: 64 (over y, z, core), lat: 4 (over x).
Axes of the slice: x: 4, y: 4, z: 8, core: 2. Of those that a mesh axis runs over, the one named last changes fastest.
Arguments:
- traj: float32 [64, 83, 24, 192], P('tm', None, 'lat'), may hold values from -6 to 6
- noise: float32 [64, 83, 24, 192], P('tm', None, 'lat'), may hold values from -6 to 6
- step_index: int32 [64], P('tm'), may hold values from 0 to 999
- embed_weight: bfloat16 [83, 512], replicated, may hold values from -0.625 to 0.625
- time_weight: float32 [512, 512], replicated, may hold values from -0.25 to 0.25
- dw_weight: float32 [512, 25], replicated, may hold values from -1.25 to 1.25
- ln_gain: float32 [512], replicated, may hold values from 0.5 to 1.5
- up_weight: bfloat16 [512, 1024], replicated, may hold values from -0.25 to 0.25
- down_weight: bfloat16 [1024, 512], replicated, may hold values from -0.1875 to 0.1875
- out_weight: bfloat16 [512, 83], replicated, may hold values from -0.25 to 0.25
Outputs:
- trajectory: float32 [64, 83, 24, 192], P('tm', None, 'lat')
All inputs are finite; a program needn't handle non-finite values.
Results may differ from a plain program's by a relative error of at most 0.0025.
Values may be sent and summed in bfloat16 or wider, within the bound.
A program may use at most 128 MiB of HBM per device.

v0:
```python
import math

import jax
import jax.numpy as jnp
from jax import lax
from jax.sharding import PartitionSpec as P

ITERS = 2
LEVELS = 1000


def with_halo(x, sides, width):
    for axis, dim in sides:
        devices, length = (lax.axis_size(axis), x.shape[dim])
        up = [(i, (i + 1) % devices) for i in range(devices - 1)]
        down = [(j, i) for i, j in up]
        last = lax.slice_in_dim(x, length - width, length, axis=dim)
        first = lax.slice_in_dim(x, 0, width, axis=dim)
        before = lax.ppermute(last, axis, up)
        after = lax.ppermute(first, axis, down)
        x = jnp.concatenate([before, x, after], axis=dim)
    return x


def entering(part, axis, combine, identity):
    place = lax.axis_index(axis)
    gathered = lax.all_gather(part, axis)
    state = jnp.zeros_like(part) + jnp.asarray(identity, part.dtype)

    def one(turn, state):
        return combine(state, lax.dynamic_index_in_dim(gathered, turn, 0, False))

    return lax.fori_loop(0, place, one, state)


def spread(value, axis, source):
    kept = jnp.where(lax.axis_index(axis) == source, value, 0).astype(value.dtype)
    return lax.psum(kept, axis)


def noise_levels(step_index):
    log_ratio = math.log(0.1) / (LEVELS - 1)
    return 2.0 * jnp.exp(step_index.astype(jnp.float32) * log_ratio)


def conditions(noise_level, time_weight):
    half_width = time_weight.shape[0] // 2
    frequency = jnp.exp(jnp.arange(half_width, dtype=jnp.float32) * (-math.log(100.0) / half_width))
    angles = jnp.log(noise_level)[:, None] * frequency[None, :]
    features = jnp.concatenate([jnp.cos(angles), jnp.sin(angles)], axis=1)
    return jax.nn.silu(jnp.dot(features, time_weight, precision=lax.Precision.HIGHEST))


def depthwise_taps(lat_padded, dw_weight):
    lat_rows = lat_padded.shape[1] - 4
    widened = lat_padded.astype(jnp.float32)
    lon_cols = widened.shape[2]
    widened = jnp.concatenate([widened[:, :, -2:], widened, widened[:, :, :2]], axis=2)
    summed = jnp.zeros((widened.shape[0], lat_rows, lon_cols), jnp.float32)
    for row_tap in range(5):
        for col_tap in range(5):
            summed = (
                summed
                + dw_weight[:, row_tap * 5 + col_tap][:, None, None]
                * widened[:, row_tap : row_tap + lat_rows, col_tap : col_tap + lon_cols]
            )
    return summed


def denoise(
    current, condition, embed_weight, dw_weight, ln_gain, up_weight, down_weight, out_weight
):
    channels, lat_rows, lon_cols = current.shape
    width = embed_weight.shape[1]
    as_rows = current.astype(jnp.bfloat16).reshape(channels, lat_rows * lon_cols)
    embedded = jnp.dot(embed_weight.T, as_rows, preferred_element_type=jnp.float32)
    activation = (embedded + condition[:, None]).astype(jnp.bfloat16)
    padded = with_halo(activation.reshape(width, lat_rows, lon_cols), (("lat", 1),), 2)
    convolved = depthwise_taps(padded, dw_weight).reshape(width, lat_rows * lon_cols)
    average = jnp.mean(convolved, axis=0)
    centred = convolved - average[None, :]
    variance = jnp.mean(centred * centred, axis=0)
    normed = (centred * lax.rsqrt(variance + 1e-06)[None, :] * ln_gain[:, None]).astype(
        jnp.bfloat16
    )
    hidden = jax.nn.gelu(
        jnp.dot(up_weight.T, normed, preferred_element_type=jnp.float32), approximate=True
    ).astype(jnp.bfloat16)
    block_out = (
        activation.astype(jnp.float32)
        + jnp.dot(down_weight.T, hidden, preferred_element_type=jnp.float32)
    ).astype(jnp.bfloat16)
    return jnp.dot(out_weight.T, block_out, preferred_element_type=jnp.float32).reshape(
        channels, lat_rows, lon_cols
    )


def add_terms(earlier, later):
    return earlier + later


def earlier_sum(increment):
    return entering(increment, "tm", add_terms, jnp.zeros_like(increment))


def shards(
    traj,
    noise,
    step_index,
    embed_weight,
    time_weight,
    dw_weight,
    ln_gain,
    up_weight,
    down_weight,
    out_weight,
):
    noise_level = noise_levels(step_index)
    condition = conditions(noise_level, time_weight)[0]
    level_now = noise_level[0]
    root = traj[0]
    anchor = spread(root, "tm", 0)
    current = root
    for picard_step in range(ITERS):
        drift_term = denoise(
            current, condition, embed_weight, dw_weight, ln_gain, up_weight, down_weight, out_weight
        )
        increment = 0.125 * level_now * drift_term + 0.125 * jnp.sqrt(level_now) * noise[0]
        current = anchor + earlier_sum(increment)
    return current[None]


def solution(mesh):
    in_specs = (
        P("tm", None, "lat", None),
        P("tm", None, "lat", None),
        P("tm"),
        P(),
        P(),
        P(),
        P(),
        P(),
        P(),
        P(),
    )
    out_specs = P("tm", None, "lat", None)
    return jax.shard_map(shards, mesh=mesh, in_specs=in_specs, out_specs=out_specs, check_vma=False)
```

profile of v0, /device:TPU:249, one launch (start us, length us, event | category | flops | bytes accessed | tf_op | source)
XLA Modules:
  0.0 650.9 jit_solution(13524946127802669461)
XLA Ops:
  7.4 1.8 fusion.162
  9.3 2.4 convert_reduce_fusion
  13.3 3.1 collective-permute-start
  16.4 1.3 collective-permute-start.1
  18.6 1.2 fusion.176
  20.1 4.1 collective-permute-done
  24.1 3.8 collective-permute-done.1
  28.5 8.8 %fusion.170 = (f32[6,192]{1,0:T(8,128)S(1)}, f32[512,6,192]{0,2,1:T(8,128)S(1)}) fusion(f32[512,10,2]{0,2,1:T(2,128)S(1)} %get-tuple-element.84, f32[512,10,192]{0,2,1:T(8,128)S(1)} %maximum_convert_fusion, f32[512]{0:T(512)S(1)} %bitcast.124, f32[512]{0:T(512)S(1)} %bitcast.126, f32[512]{0:T(512)S(1)} %bitcast.130, ...), kind=kLoop, calls=%fused_computation.285 | loop fusion | flops 41286528 | bytes 18225664 | tf_op jit(solution)/shard_map/reduce_sum | solution.py:80
  39.1 3.5 fusion.9
  42.7 4.5 fusion.24
  47.2 1.3 mul.669
  50.6 142.0 %all-gather.3.cloned.1.call-done = f32[64,83,6,192]{3,1,2,0:T(8,128)} async-done(((f32[1,83,6,192]{3,1,2,0:T(8,128)}), f32[64,83,6,192]{3,1,2,0:T(8,128)}) %all-gather.3.cloned.1.call-update) | async-done | bytes 24477712 | tf_op jit(solution)/shard_map/all_gather | solution.py:27
  192.7 88.0 %while.20 = (s32[]{:T(128)}, f32[83,6,192]{2,1,0:T(8,128)S(1)}, s32[]{:T(128)}, f32[64,83,6,192]{3,1,2,0:T(8,128)}, s32[]{:T(128)}, /*index=5*/s32[]{:T(128)}, s32[]{:T(128)}) while((s32[]{:T(128)}, f32[83,6,192]{2,1,0:T(8,128)S(1)}, s32[]{:T(128)}, f32[64,83,6,192]{3,1,2,0:T(8,128)}, s32[]{:T(128)}, /*index=5*/s32[]{:T(128)}, s32[]{:T(128)}) %tuple.63), condition=%wide.region_4.5_spmd, body=%wide.region_3.4_spmd.sunk | while | flops 95621 | bytes 1912435 | solution.py:33
  196.9 1.1 constant_dynamic-slice_fusion.4
  198.3 1.1 constant_dynamic-slice_fusion.4
  199.6 1.1 constant_dynamic-slice_fusion.4
  201.0 1.1 constant_dynamic-slice_fusion.4
  206.6 1.1 constant_dynamic-slice_fusion.4
  208.0 1.1 constant_dynamic-slice_fusion.4
  209.4 1.1 constant_dynamic-slice_fusion.4
  210.8 1.1 constant_dynamic-slice_fusion.4
  213.6 1.1 constant_dynamic-slice_fusion.4
  215.0 1.1 constant_dynamic-slice_fusion.4
  216.4 1.1 constant_dynamic-slice_fusion.4
  219.2 1.1 constant_dynamic-slice_fusion.4
  220.6 1.1 constant_dynamic-slice_fusion.4
  222.0 1.1 constant_dynamic-slice_fusion.4
  223.4 1.1 constant_dynamic-slice_fusion.4
  224.7 1.1 constant_dynamic-slice_fusion.4
  226.1 1.1 constant_dynamic-slice_fusion.4
  227.5 1.1 constant_dynamic-slice_fusion.4
  230.3 1.1 constant_dynamic-slice_fusion.4
  231.7 1.1 constant_dynamic-slice_fusion.4
  233.1 1.1 constant_dynamic-slice_fusion.4
  237.3 1.1 constant_dynamic-slice_fusion.4
  238.7 1.1 constant_dynamic-slice_fusion.4
  242.9 1.1 constant_dynamic-slice_fusion.4
  244.3 1.1 constant_dynamic-slice_fusion.4
  245.7 1.1 constant_dynamic-slice_fusion.4
  247.1 1.1 constant_dynamic-slice_fusion.4
  248.5 1.1 constant_dynamic-slice_fusion.4
  249.9 1.1 constant_dynamic-slice_fusion.4
  251.2 1.1 constant_dynamic-slice_fusion.4
  262.4 1.1 constant_dynamic-slice_fusion.4
  263.8 1.1 constant_dynamic-slice_fusion.4
  265.2 1.1 constant_dynamic-slice_fusion.4
  270.8 1.1 constant_dynamic-slice_fusion.4
  272.2 1.1 constant_dynamic-slice_fusion.4
  273.6 1.1 constant_dynamic-slice_fusion.4
  274.9 1.1 constant_dynamic-slice_fusion.4
  277.7 1.1 constant_dynamic-slice_fusion.4
  280.7 94.8 %all-reduce.2.cloned.1.call-done = f32[83,6,192]{2,0,1:T(8,128)} async-done(((f32[83,6,192]{2,0,1:T(8,128)}), f32[83,6,192]{2,0,1:T(8,128)}) %all-reduce.2.cloned.1.call-update) | async-done | bytes 382480 | tf_op jit(solution)/shard_map/psum | solution.py:38
  375.5 1.2 fusion.160
  377.7 3.1 collective-permute-start.2
  381.0 1.3 collective-permute-start.3
  382.3 7.1 %collective-permute-done.2 = bf16[512,2,192]{0,2,1:T(8,128)(2,1)S(1)} collective-permute-done((bf16[512,2,192]{0,2,1:T(8,128)(2,1)S(1)}, bf16[512,2,192]{0,2,1:T(8,128)(2,1)S(1)}, u32[]{:S(2)}, u32[]{:S(2)}) %collective-permute-start.2) | collective-permute-done | bytes 393248 | tf_op jit(solution)/shard_map/ppermute | solution.py:19
  389.4 4.0 collective-permute-done.3
  393.9 8.8 %fusion.168 = (f32[6,192]{1,0:T(8,128)S(1)}, f32[512,6,192]{0,2,1:T(8,128)S(1)}) fusion(f32[512,10,2]{0,2,1:T(2,128)S(1)} %get-tuple-element.82, f32[512,10,192]{0,2,1:T(8,128)S(1)} %maximum_convert_fusion.1, f32[512]{0:T(512)S(1)} %bitcast.125, f32[512]{0:T(512)S(1)} %bitcast.127, f32[512]{0:T(512)S(1)} %bitcast.131, ...), kind=kLoop, calls=%fused_computation.284 | loop fusion | flops 41286528 | bytes 18225664 | tf_op jit(solution)/shard_map/reduce_sum | solution.py:80
  403.9 3.5 fusion.17
  407.4 3.7 fusion.25
  412.5 142.4 %all-gather.5.cloned.1.call-done = f32[64,83,6,192]{3,1,2,0:T(8,128)} async-done(((f32[1,83,6,192]{3,1,2,0:T(8,128)}), f32[64,83,6,192]{3,1,2,0:T(8,128)}) %all-gather.5.cloned.1.call-update) | async-done | bytes 24477712 | tf_op jit(solution)/shard_map/all_gather | solution.py:27
  555.0 87.8 %while.21 = (s32[]{:T(128)}, f32[83,6,192]{2,1,0:T(8,128)S(1)}, s32[]{:T(128)}, f32[64,83,6,192]{3,1,2,0:T(8,128)}, s32[]{:T(128)}, /*index=5*/s32[]{:T(128)}, s32[]{:T(128)}) while((s32[]{:T(128)}, f32[83,6,192]{2,1,0:T(8,128)S(1)}, s32[]{:T(128)}, f32[64,83,6,192]{3,1,2,0:T(8,128)}, s32[]{:T(128)}, /*index=5*/s32[]{:T(128)}, s32[]{:T(128)}) %tuple.66), condition=%wide.region_8.9_spmd, body=%wide.region_7.8_spmd.sunk | while | flops 95621 | bytes 1912435 | solution.py:33
  555.0 1.1 constant_dynamic-slice_fusion.5
  643.0 1.3 copy.34
  (353 shorter events, 139.4 us)
Async XLA Ops:
  6.5 32.6 %copy-start = (bf16[512,1024]{1,0:T(8,128)(2,1)S(1)}, bf16[512,1024]{1,0:T(8,128)(2,1)}, u32[]{:S(2)}) copy-start(bf16[512,1024]{1,0:T(8,128)(2,1)} %param.21) | copy-start | bytes 3145732
  6.5 5.5 copy-start.9
  6.5 186.1 %all-gather.3.cloned.1.call-start = ((), (), s32[]{:S(2)}) async-start(), calls=%async_computation.1 | async-start | bytes 35143680 | tf_op jit(solution)/shard_map/all_gather | solution.py:27
  9.3 2.7 copy-start.44
  12.6 15.7 %copy-start.3 = (bf16[512,1152]{1,0:T(8,128)(2,1)}, bf16[512,1152]{1,0:T(8,128)(2,1)S(1)}, u32[]{:S(2)}) copy-start(bf16[512,1152]{1,0:T(8,128)(2,1)S(1)} %fusion.22) | copy-start | bytes 3538948
  13.3 10.9 %collective-permute-start = (bf16[512,2,192]{0,2,1:T(8,128)(2,1)S(1)}, bf16[512,2,192]{0,2,1:T(8,128)(2,1)S(1)}, u32[]{:S(2)}, u32[]{:S(2)}) collective-permute-start(bf16[512,2,192]{0,2,1:T(8,128)(2,1)S(1)} %get-tuple-element.87), channel_id=1, source_target_pairs={{0,1},{1,2},{2,3},{4,5},{5,6},{6,7},{8,9},{9,10},{10,11},{12,13},{... | collective-permute-start | bytes 1179656 | tf_op jit(solution)/shard_map/ppermute | solution.py:19
  16.4 11.6 %collective-permute-start.1 = (bf16[512,2,192]{0,2,1:T(8,128)(2,1)S(1)}, bf16[512,2,192]{0,2,1:T(8,128)(2,1)S(1)}, u32[]{:S(2)}, u32[]{:S(2)}) collective-permute-start(bf16[512,2,192]{0,2,1:T(8,128)(2,1)S(1)} %get-tuple-element.88), channel_id=1, source_target_pairs={{1,0},{2,1},{3,2},{5,4},{6,5},{7,6},{9,8},{10,9},{11,10},{13,12},{... | collective-permute-start | bytes 1179656 | tf_op jit(solution)/shard_map/ppermute | solution.py:20
  19.9 8.4 %copy-start.10 = (f32[512,1]{0,1:T(1,128)}, f32[512,1]{0,1:T(1,128)S(1)}, u32[]{:S(2)}) copy-start(f32[512,1]{0,1:T(1,128)S(1)} %get-tuple-element.91) | copy-start | bytes 6148
  19.9 8.4 %copy-start.12 = (f32[512,1]{0,1:T(1,128)}, f32[512,1]{0,1:T(1,128)S(1)}, u32[]{:S(2)}) copy-start(f32[512,1]{0,1:T(1,128)S(1)} %get-tuple-element.92) | copy-start | bytes 6148
  19.9 8.4 %copy-start.14 = (f32[512,1]{0,1:T(1,128)}, f32[512,1]{0,1:T(1,128)S(1)}, u32[]{:S(2)}) copy-start(f32[512,1]{0,1:T(1,128)S(1)} %get-tuple-element.93) | copy-start | bytes 6148
  19.9 8.4 %copy-start.16 = (f32[512,1]{0,1:T(1,128)}, f32[512,1]{0,1:T(1,128)S(1)}, u32[]{:S(2)}) copy-start(f32[512,1]{0,1:T(1,128)S(1)} %get-tuple-element.94) | copy-start | bytes 6148
  19.9 8.4 %copy-start.18 = (f32[512,1]{0,1:T(1,128)}, f32[512,1]{0,1:T(1,128)S(1)}, u32[]{:S(2)}) copy-start(f32[512,1]{0,1:T(1,128)S(1)} %get-tuple-element.95) | copy-start | bytes 6148
  19.9 8.4 %copy-start.20 = (f32[512,1]{0,1:T(1,128)}, f32[512,1]{0,1:T(1,128)S(1)}, u32[]{:S(2)}) copy-start(f32[512,1]{0,1:T(1,128)S(1)} %get-tuple-element.96) | copy-start | bytes 6148
  20.0 8.4 %copy-start.22 = (f32[512,1]{0,1:T(1,128)}, f32[512,1]{0,1:T(1,128)S(1)}, u32[]{:S(2)}) copy-start(f32[512,1]{0,1:T(1,128)S(1)} %get-tuple-element.97) | copy-start | bytes 6148
  20.0 8.4 %copy-start.24 = (f32[512,1]{0,1:T(1,128)}, f32[512,1]{0,1:T(1,128)S(1)}, u32[]{:S(2)}) copy-start(f32[512,1]{0,1:T(1,128)S(1)} %get-tuple-element.98) | copy-start | bytes 6148
  20.0 8.4 %copy-start.26 = (f32[512,1]{0,1:T(1,128)}, f32[512,1]{0,1:T(1,128)S(1)}, u32[]{:S(2)}) copy-start(f32[512,1]{0,1:T(1,128)S(1)} %get-tuple-element.99) | copy-start | bytes 6148
  20.0 8.4 %copy-start.28 = (f32[512,1]{0,1:T(1,128)}, f32[512,1]{0,1:T(1,128)S(1)}, u32[]{:S(2)}) copy-start(f32[512,1]{0,1:T(1,128)S(1)} %get-tuple-element.100) | copy-start | bytes 6148
  20.0 8.4 %copy-start.30 = (f32[512,1]{0,1:T(1,128)}, f32[512,1]{0,1:T(1,128)S(1)}, u32[]{:S(2)}) copy-start(f32[512,1]{0,1:T(1,128)S(1)} %get-tuple-element.101) | copy-start | bytes 6148
  20.0 8.4 %copy-start.32 = (f32[512,1]{0,1:T(1,128)}, f32[512,1]{0,1:T(1,128)S(1)}, u32[]{:S(2)}) copy-start(f32[512,1]{0,1:T(1,128)S(1)} %get-tuple-element.102) | copy-start | bytes 6148
  20.0 8.4 %copy-start.34 = (f32[512,1]{0,1:T(1,128)}, f32[512,1]{0,1:T(1,128)S(1)}, u32[]{:S(2)}) copy-start(f32[512,1]{0,1:T(1,128)S(1)} %get-tuple-element.103) | copy-start | bytes 6148
  20.0 8.4 %copy-start.36 = (f32[512,1]{0,1:T(1,128)}, f32[512,1]{0,1:T(1,128)S(1)}, u32[]{:S(2)}) copy-start(f32[512,1]{0,1:T(1,128)S(1)} %get-tuple-element.104) | copy-start | bytes 6148
  20.0 8.4 %copy-start.38 = (f32[512,1]{0,1:T(1,128)}, f32[512,1]{0,1:T(1,128)S(1)}, u32[]{:S(2)}) copy-start(f32[512,1]{0,1:T(1,128)S(1)} %get-tuple-element.105) | copy-start | bytes 6148
  20.0 8.4 %copy-start.40 = (f32[512,1]{0,1:T(1,128)}, f32[512,1]{0,1:T(1,128)S(1)}, u32[]{:S(2)}) copy-start(f32[512,1]{0,1:T(1,128)S(1)} %get-tuple-element.106) | copy-start | bytes 6148
  20.1 8.4 %copy-start.42 = (f32[512,1]{0,1:T(1,128)}, f32[512,1]{0,1:T(1,128)S(1)}, u32[]{:S(2)}) copy-start(f32[512,1]{0,1:T(1,128)S(1)} %get-tuple-element.107) | copy-start | bytes 6148
  39.1 3.6 copy-start.4
  39.1 3.6 copy-start.47
  42.7 5.8 copy-start.6
  47.2 2.5 copy-start.8
  49.6 325.9 %all-reduce.2.cloned.1.call-start = ((), (), s32[]{:S(2)}) async-start(), calls=%async_computation | async-start | bytes 1081344 | tf_op jit(solution)/shard_map/psum | solution.py:38
  50.6 504.3 %all-gather.5.cloned.1.call-start = ((), (), s32[]{:S(2)}) async-start(), calls=%async_computation.2 | async-start | bytes 35143680 | tf_op jit(solution)/shard_map/all_gather | solution.py:27
  280.7 96.4 %copy-start.45 = (f32[512]{0:T(512)S(1)}, f32[512]{0:T(512)}, u32[]{:S(2)}) copy-start(f32[512]{0:T(512)} %copy-done.44) | copy-start | bytes 6148
  377.6 16.1 %copy-start.1 = (bf16[1152,512]{1,0:T(8,128)(2,1)}, bf16[1152,512]{1,0:T(8,128)(2,1)S(1)}, u32[]{:S(2)}) copy-start(bf16[1152,512]{1,0:T(8,128)(2,1)S(1)} %fusion.23) | copy-start | bytes 3538948
  377.7 11.7 %collective-permute-start.2 = (bf16[512,2,192]{0,2,1:T(8,128)(2,1)S(1)}, bf16[512,2,192]{0,2,1:T(8,128)(2,1)S(1)}, u32[]{:S(2)}, u32[]{:S(2)}) collective-permute-start(bf16[512,2,192]{0,2,1:T(8,128)(2,1)S(1)} %get-tuple-element.85), channel_id=1, source_target_pairs={{0,1},{1,2},{2,3},{4,5},{5,6},{6,7},{8,9},{9,10},{10,11},{12,13},{... | collective-permute-start | bytes 1179656 | tf_op jit(solution)/shard_map/ppermute | solution.py:19
  380.8 12.9 %copy-start.11 = (f32[512,1]{0,1:T(1,128)S(1)}, f32[512,1]{0,1:T(1,128)}, u32[]{:S(2)}) copy-start(f32[512,1]{0,1:T(1,128)} %copy-done.10) | copy-start | bytes 6148
  380.8 12.9 %copy-start.13 = (f32[512,1]{0,1:T(1,128)S(1)}, f32[512,1]{0,1:T(1,128)}, u32[]{:S(2)}) copy-start(f32[512,1]{0,1:T(1,128)} %copy-done.12) | copy-start | bytes 6148
  380.8 12.9 %copy-start.15 = (f32[512,1]{0,1:T(1,128)S(1)}, f32[512,1]{0,1:T(1,128)}, u32[]{:S(2)}) copy-start(f32[512,1]{0,1:T(1,128)} %copy-done.14) | copy-start | bytes 6148
  380.8 12.9 %copy-start.17 = (f32[512,1]{0,1:T(1,128)S(1)}, f32[512,1]{0,1:T(1,128)}, u32[]{:S(2)}) copy-start(f32[512,1]{0,1:T(1,128)} %copy-done.16) | copy-start | bytes 6148
  380.8 12.9 %copy-start.19 = (f32[512,1]{0,1:T(1,128)S(1)}, f32[512,1]{0,1:T(1,128)}, u32[]{:S(2)}) copy-start(f32[512,1]{0,1:T(1,128)} %copy-done.18) | copy-start | bytes 6148
  380.8 12.9 %copy-start.21 = (f32[512,1]{0,1:T(1,128)S(1)}, f32[512,1]{0,1:T(1,128)}, u32[]{:S(2)}) copy-start(f32[512,1]{0,1:T(1,128)} %copy-done.20) | copy-start | bytes 6148
  380.9 12.9 %copy-start.23 = (f32[512,1]{0,1:T(1,128)S(1)}, f32[512,1]{0,1:T(1,128)}, u32[]{:S(2)}) copy-start(f32[512,1]{0,1:T(1,128)} %copy-done.22) | copy-start | bytes 6148
  380.9 12.9 %copy-start.25 = (f32[512,1]{0,1:T(1,128)S(1)}, f32[512,1]{0,1:T(1,128)}, u32[]{:S(2)}) copy-start(f32[512,1]{0,1:T(1,128)} %copy-done.24) | copy-start | bytes 6148
  380.9 12.9 %copy-start.27 = (f32[512,1]{0,1:T(1,128)S(1)}, f32[512,1]{0,1:T(1,128)}, u32[]{:S(2)}) copy-start(f32[512,1]{0,1:T(1,128)} %copy-done.26) | copy-start | bytes 6148
  380.9 12.9 %copy-start.29 = (f32[512,1]{0,1:T(1,128)S(1)}, f32[512,1]{0,1:T(1,128)}, u32[]{:S(2)}) copy-start(f32[512,1]{0,1:T(1,128)} %copy-done.28) | copy-start | bytes 6148
  380.9 12.9 %copy-start.31 = (f32[512,1]{0,1:T(1,128)S(1)}, f32[512,1]{0,1:T(1,128)}, u32[]{:S(2)}) copy-start(f32[512,1]{0,1:T(1,128)} %copy-done.30) | copy-start | bytes 6148
  380.9 12.9 %copy-start.33 = (f32[512,1]{0,1:T(1,128)S(1)}, f32[512,1]{0,1:T(1,128)}, u32[]{:S(2)}) copy-start(f32[512,1]{0,1:T(1,128)} %copy-done.32) | copy-start | bytes 6148
  380.9 12.9 %copy-start.35 = (f32[512,1]{0,1:T(1,128)S(1)}, f32[512,1]{0,1:T(1,128)}, u32[]{:S(2)}) copy-start(f32[512,1]{0,1:T(1,128)} %copy-done.34) | copy-start | bytes 6148
  380.9 12.9 %copy-start.37 = (f32[512,1]{0,1:T(1,128)S(1)}, f32[512,1]{0,1:T(1,128)}, u32[]{:S(2)}) copy-start(f32[512,1]{0,1:T(1,128)} %copy-done.36) | copy-start | bytes 6148
  380.9 12.9 %copy-start.39 = (f32[512,1]{0,1:T(1,128)S(1)}, f32[512,1]{0,1:T(1,128)}, u32[]{:S(2)}) copy-start(f32[512,1]{0,1:T(1,128)} %copy-done.38) | copy-start | bytes 6148
  380.9 12.9 %copy-start.41 = (f32[512,1]{0,1:T(1,128)S(1)}, f32[512,1]{0,1:T(1,128)}, u32[]{:S(2)}) copy-start(f32[512,1]{0,1:T(1,128)} %copy-done.40) | copy-start | bytes 6148
  381.0 12.9 %copy-start.43 = (f32[512,1]{0,1:T(1,128)S(1)}, f32[512,1]{0,1:T(1,128)}, u32[]{:S(2)}) copy-start(f32[512,1]{0,1:T(1,128)} %copy-done.42) | copy-start | bytes 6148
  381.0 12.4 %collective-permute-start.3 = (bf16[512,2,192]{0,2,1:T(8,128)(2,1)S(1)}, bf16[512,2,192]{0,2,1:T(8,128)(2,1)S(1)}, u32[]{:S(2)}, u32[]{:S(2)}) collective-permute-start(bf16[512,2,192]{0,2,1:T(8,128)(2,1)S(1)} %get-tuple-element.86), channel_id=1, source_target_pairs={{1,0},{2,1},{3,2},{5,4},{6,5},{7,6},{9,8},{10,9},{11,10},{13,12},{... | collective-permute-start | bytes 1179656 | tf_op jit(solution)/shard_map/ppermute | solution.py:20
  402.7 0.7 copy-start.46
  403.9 3.6 copy-start.2
  403.9 3.6 copy-start.48
  407.4 4.0 copy-start.7
  555.0 87.8 %copy-start.5 = (f32[83,6,192]{2,0,1:T(8,128)S(1)}, f32[83,6,192]{2,0,1:T(8,128)}, u32[]{:S(2)}) copy-start(f32[83,6,192]{2,0,1:T(8,128)} %all-reduce.2.cloned.1.call-done) | copy-start | bytes 1147396
Sparse Core Ops, SparseCore 0:
  49.8 142.7 all-gather.2
  196.1 179.3 all-reduce.1
  412.7 142.2 all-gather.4
where the time goes:
time: 657 us; the launch traced here: 651 us
  waiting for transfers between devices  398 us (61%)
  local copies, waits for them, and re-layouts  146 us (22%)
  other arithmetic  59.8 us (9%)
  matrix products  18.1 us (3%)
  between operations  14.9 us (2%)
  starting transfers between devices  8.93 us (1%)
    all_gather x2, waiting for transfers between devices, entering(): gathered = lax.all_gather(part, axis)  284 us
    dynamic_slice x126, local copies, waits for them, and re-layouts, one(): return combine(state, lax.dynamic_index_in_dim(gathered, turn, 0, False))  137 us
    psum x1, waiting for transfers between devices, spread(): return lax.psum(kept, axis)  94.8 us
    add x126, other arithmetic, add_terms(): return earlier + later  34 us
    reduce_sum x2, other arithmetic, denoise(): average = jnp.mean(convolved, axis=0)  17.7 us
  transfers between devices with their start and end apart: 7, of which 7 were waited for; matrix products, arithmetic and copies ran while one was open for 14% of the time, Pallas kernels for 0%

commit v1 on v0

v1 whole, which is shorter than its diff:
```python
import functools
import math

import jax
import jax.numpy as jnp
from jax import lax
from jax.experimental import pallas as pl
from jax.experimental.pallas import tpu as pltpu
from jax.sharding import PartitionSpec as P

MESH = pl.DeviceIdType.MESH
BF, F32 = jnp.bfloat16, jnp.float32
ITERS = 2
LEVELS = 1000
NCH, NROW, NLON = 83, 6, 192
SEG, COL = 8, 24
NT = 64
CHUNKS, TILES = 3, 18
OWNERS = CHUNKS * TILES
RET = (BF, F32)
D, FF = 512, 1024


def to_tiles(ref, lead, value):
    for lane in range(3):
        for group in range(6):
            ref[lead + (lane * 6 + group,)] = value[group * 16 : group * 16 + 16, lane * 128 : lane * 128 + 128]


def from_tiles(ref, lead):
    lanes = []
    for lane in range(3):
        lanes.append(jnp.concatenate([ref[lead + (lane * 6 + group,)].astype(F32) for group in range(6)], axis=0))
    return jnp.concatenate(lanes, axis=1)


def kernel(
    traj, noise, step, emb, timew, dw, gain, up_h, down_h, outw, out,
    up, down, act, wb, conv, vt, dt, nz, condb,
    ob, inb, retb0, retb1, st, stf, halo, rsrc, rbuf,
    wsem, osend, isem, rsend, stsem, hsend, hrecv, rootsend, rootrecv,
):
    t, l = lax.axis_index("tm"), lax.axis_index("lat")

    cup = pltpu.make_async_copy(up_h, up, wsem.at[0])
    cdown = pltpu.make_async_copy(down_h, down, wsem.at[1])
    cup.start()
    cdown.start()

    barrier = pltpu.get_barrier_semaphore()

    def greet(k, _):
        pl.semaphore_signal(barrier, inc=1, device_id={"tm": lax.rem(t + k, NT)}, device_id_type=MESH)
        return 0

    lax.fori_loop(1, NT, greet, 0)

    for shift in (1, 3):
        pl.semaphore_signal(barrier, inc=1, device_id={"lat": lax.rem(l + shift, 4)}, device_id_type=MESH)

    pad = jnp.zeros((96 - NCH, 384), F32)
    for b in range(CHUNKS):
        pair = jnp.concatenate([traj[0, :, 2 * b, :], traj[0, :, 2 * b + 1, :]], axis=1)
        dt[0:NCH, :] = pair
        dt[NCH:96, :] = pad
        whole = dt[0:96, :]
        to_tiles(rsrc.at[b], (), whole)
        to_tiles(st, (0, b), whole.astype(BF))
        nz[b, 0:NCH, :] = jnp.concatenate([noise[0, :, 2 * b, :], noise[0, :, 2 * b + 1, :]], axis=1)
        nz[b, NCH:96, :] = pad

    stepf = jnp.full((8, 512), step[0].astype(F32), F32)
    level = 2.0 * jnp.exp(stepf * (math.log(0.1) / (LEVELS - 1)))
    j = lax.broadcasted_iota(jnp.int32, (8, 512), 1)
    jj = jnp.where(j < 256, j, j - 256).astype(F32)
    frequency = jnp.exp(jj * (-math.log(100.0) / 256))
    angles = jnp.log(level) * frequency
    features = jnp.where(j < 256, jnp.cos(angles), jnp.sin(angles))
    cond = jnp.dot(features, timew[...], precision=lax.Precision.HIGHEST, preferred_element_type=F32)
    condb[...] = cond * (1.0 / (1.0 + jnp.exp(-cond)))
    drift_scale = 0.125 * level[0:1, 0:384]
    noise_scale = 0.125 * jnp.sqrt(level[0:1, 0:384])

    taps = jnp.transpose(dw[...])
    for k in range(25):
        wb[k] = jnp.broadcast_to(taps[k : k + 1, :], (8, D))

    pl.semaphore_wait(barrier, NT + 1)

    def halo_up(it):
        return pltpu.make_async_remote_copy(
            src_ref=st.at[it, 0], dst_ref=halo.at[it, 1], send_sem=hsend.at[it, 0], recv_sem=hrecv.at[it, 1],
            device_id={"lat": l - 1}, device_id_type=MESH)

    def halo_down(it):
        return pltpu.make_async_remote_copy(
            src_ref=st.at[it, 2], dst_ref=halo.at[it, 0], send_sem=hsend.at[it, 1], recv_sem=hrecv.at[it, 0],
            device_id={"lat": l + 1}, device_id_type=MESH)

    def start_up(it):
        @pl.when(l > 0)
        def _():
            halo_up(it).start()

    def start_down(it):
        @pl.when(l < 3)
        def _():
            halo_down(it).start()

    start_up(0)
    start_down(0)

    def root_copy(k):
        return pltpu.make_async_remote_copy(
            src_ref=rsrc.at[k % 3, k // 3], dst_ref=rbuf, send_sem=rootsend, recv_sem=rootrecv,
            device_id={"tm": k}, device_id_type=MESH)

    @pl.when(t == 0)
    def _():
        pltpu.make_async_copy(rsrc.at[0, 0], rbuf, rootrecv).start()

        def one(k, _):
            root_copy(k).start()
            return 0

        lax.fori_loop(1, OWNERS, one, 0)

    def embed(read, row0):
        vt[:, 0:96] = jnp.transpose(read)

        for rr in range(2):
            cols = [vt[pl.ds(rr * NLON + c, SEG, stride=COL), :] for c in range(COL)]
            lhs = jnp.concatenate(cols, axis=0)[:, 0:NCH].astype(BF)
            value = jnp.dot(lhs, emb[...], preferred_element_type=F32)
            value = value.reshape(COL, SEG, D) + condb[...][None]
            value = value.astype(BF).astype(F32)
            act[row0 + rr, 2 : 2 + COL] = value
            for c in range(2):
                act[row0 + rr, c] = pltpu.roll(value[COL - 2 + c], 1, 0)
                act[row0 + rr, COL + 2 + c] = pltpu.roll(value[c], SEG - 1, 0)

    def zero_rows(row0):
        act[pl.ds(row0, 2)] = jnp.zeros((2, COL + 4, SEG, D), F32)

    def convolve(b):
        for g in range(4):
            lanes = slice(g * 128, g * 128 + 128)

            def block(cb, _):
                c0 = cb * 4
                acc = [[None] * 4 for _ in range(2)]
                for ri in range(6):
                    xs = [act[2 * b + ri, c0 + ci, :, lanes] for ci in range(8)]
                    for rr in range(2):
                        tap = ri - rr
                        if not 0 <= tap < 5:
                            continue
                        for cc in range(4):
                            for tj in range(5):
                                term = wb[tap * 5 + tj, :, lanes] * xs[cc + tj]
                                acc[rr][cc] = term if acc[rr][cc] is None else acc[rr][cc] + term
                for rr in range(2):
                    for cc in range(4):
                        conv[rr, c0 + cc, :, lanes] = acc[rr][cc]
                return 0

            lax.fori_loop(0, 6, block, 0)

    def mlp(b):
        for rr in range(2):
            x = conv[rr].reshape(NLON, D)
            mean = jnp.mean(x, axis=1, keepdims=True)
            x = x - mean
            var = jnp.mean(x * x, axis=1, keepdims=True)
            normed = (x * lax.rsqrt(var + 1e-6) * gain[...]).astype(BF)
            h = jnp.dot(normed, up[...], preferred_element_type=F32)
            inner = 0.7978845608028654 * (h + 0.044715 * (h * h * h))
            hidden = (0.5 * h * (1.0 + jnp.tanh(inner))).astype(BF)
            y = jnp.dot(hidden, down[...], preferred_element_type=F32)
            y = (act[2 + 2 * b + rr, 2 : 2 + COL].reshape(NLON, D) + y).astype(BF)
            drift = jnp.dot(y, outw[...], preferred_element_type=F32)
            for c in range(COL):
                vt[pl.ds(rr * NLON + c, SEG, stride=COL), 0:NCH] = drift[c * SEG : c * SEG + SEG, :]
        dT = jnp.transpose(vt[...])[0:96, :]
        return drift_scale * dT + noise_scale * nz[b]

    def send_chunk(it, b):
        def one(k, _):
            owner = 3 * k + b

            @pl.when(owner == t)
            def _():
                pltpu.make_async_copy(ob.at[it, b, k], inb.at[it, t], isem.at[it]).start()

            @pl.when(owner != t)
            def _():
                pltpu.make_async_remote_copy(
                    src_ref=ob.at[it, b, k], dst_ref=inb.at[it, t], send_sem=osend.at[it, b], recv_sem=isem.at[it],
                    device_id={"tm": owner}, device_id_type=MESH).start()

            return 0

        lax.fori_loop(0, TILES, one, 0)

    mine_b, mine_k = lax.rem(t, 3), t // 3

    def scan(it):
        retb = (retb0, retb1)[it]
        dst = (st.at[1], stf)[it]

        @pl.when(t < OWNERS)
        def _():
            if it == 0:
                pltpu.make_async_copy(rbuf, rbuf, rootrecv).wait()
            pltpu.make_async_copy(inb.at[it], inb.at[it], isem.at[it]).wait()

            def one(s, acc):
                retb[s] = acc.astype(retb.dtype)

                @pl.when(s == t)
                def _():
                    pltpu.make_async_copy(retb.at[s], dst.at[mine_b, mine_k], stsem.at[it, mine_b]).start()

                @pl.when(s != t)
                def _():
                    pltpu.make_async_remote_copy(
                        src_ref=retb.at[s], dst_ref=dst.at[mine_b, mine_k], send_sem=rsend.at[it],
                        recv_sem=stsem.at[it, mine_b], device_id={"tm": s}, device_id_type=MESH).start()

                return acc + inb[it, s].astype(F32)

            lax.fori_loop(0, NT, one, rbuf[...])

    def wait_chunk(it, b):
        dst = (st.at[1], stf)[it]
        pltpu.make_async_copy(dst.at[b], dst.at[b], stsem.at[it, b]).wait()

    cup.wait()
    cdown.wait()
    vt[...] = jnp.zeros(vt.shape, F32)
    for it in range(ITERS):
        if it == 1:
            wait_chunk(0, 0)
            start_up(1)
            wait_chunk(0, 2)
            start_down(1)
            wait_chunk(0, 1)
        for b in range(CHUNKS):
            embed(from_tiles(st, (it, b)), 2 + 2 * b)
        for b in (1, 0, 2):
            if b == 0:
                @pl.when(l > 0)
                def _():
                    halo_up(it).wait_send()
                    pltpu.make_async_copy(halo.at[it, 0], halo.at[it, 0], hrecv.at[it, 0]).wait()
                    embed(from_tiles(halo, (it, 0)), 0)

                @pl.when(l == 0)
                def _():
                    zero_rows(0)
            if b == 2:
                @pl.when(l < 3)
                def _():
                    halo_down(it).wait_send()
                    pltpu.make_async_copy(halo.at[it, 1], halo.at[it, 1], hrecv.at[it, 1]).wait()
                    embed(from_tiles(halo, (it, 1)), 8)

                @pl.when(l == 3)
                def _():
                    zero_rows(8)
            convolve(b)
            to_tiles(ob, (it, b), mlp(b).astype(BF))
            send_chunk(it, b)
        scan(it)

    for b in (1, 0, 2):
        wait_chunk(1, b)
        value = from_tiles(stf, (b,))[0:NCH, :]
        out[0, :, 2 * b, :] = value[:, 0:NLON]
        out[0, :, 2 * b + 1, :] = value[:, NLON : 2 * NLON]

    def drain(ref, sem):
        pltpu.make_async_copy(ref, ref, sem).wait()

    @pl.when(t == 0)
    def _():
        drain(rsrc.at[0], rootsend)
        drain(rsrc.at[1], rootsend)
        drain(rsrc.at[2, pl.ds(0, TILES - 1)], rootsend)

    for it in range(ITERS):
        for b in range(CHUNKS):
            own = jnp.logical_and(mine_b == b, t < OWNERS)

            @pl.when(own)
            def _():
                drain(ob.at[it, b, pl.ds(0, TILES - 1)], osend.at[it, b])

            @pl.when(jnp.logical_not(own))
            def _():
                drain(ob.at[it, b], osend.at[it, b])

        @pl.when(t < OWNERS)
        def _():
            retb = (retb0, retb1)[it]
            drain(retb.at[pl.ds(0, NT - 1)], rsend.at[it])


def shards(traj, noise, step_index, emb, timew, dw, gain, up, down, outw):
    vm = pl.BlockSpec(memory_space=pltpu.VMEM)
    anyspace = pl.BlockSpec(memory_space=pl.ANY)
    dma = pltpu.SemaphoreType.DMA
    return pl.pallas_call(
        kernel,
        out_shape=jax.ShapeDtypeStruct((1, NCH, NROW, NLON), F32),
        in_specs=[vm, vm, pl.BlockSpec(memory_space=pltpu.SMEM), vm, vm, vm, vm, anyspace, anyspace, vm],
        out_specs=vm,
        scratch_shapes=[
            pltpu.VMEM((D, FF), BF),
            pltpu.VMEM((FF, D), BF),
            pltpu.VMEM((10, COL + 4, SEG, D), F32),
            pltpu.VMEM((25, 8, D), F32),
            pltpu.VMEM((2, COL, SEG, D), F32),
            pltpu.VMEM((384, 128), F32),
            pltpu.VMEM((96, 384), F32),
            pltpu.VMEM((CHUNKS, 96, 384), F32),
            pltpu.VMEM((8, D), F32),
            pltpu.VMEM((ITERS, CHUNKS, TILES, 16, 128), BF),
            pltpu.VMEM((ITERS, NT, 16, 128), BF),
            pltpu.VMEM((NT, 16, 128), RET[0]),
            pltpu.VMEM((NT, 16, 128), RET[1]),
            pltpu.VMEM((ITERS, CHUNKS, TILES, 16, 128), BF),
            pltpu.VMEM((CHUNKS, TILES, 16, 128), RET[1]),
            pltpu.VMEM((ITERS, 2, TILES, 16, 128), BF),
            pltpu.VMEM((CHUNKS, TILES, 16, 128), F32),
            pltpu.VMEM((16, 128), F32),
            dma((2,)),
            dma((ITERS, CHUNKS)),
            dma((ITERS,)),
            dma((ITERS,)),
            dma((ITERS, CHUNKS)),
            dma((ITERS, 2)),
            dma((ITERS, 2)),
            dma,
            dma,
        ],
        compiler_params=pltpu.CompilerParams(
            collective_id=0, has_side_effects=True, vmem_limit_bytes=56 * 2**20
        ),
    )(traj, noise, step_index, emb, timew, dw, gain.reshape(1, D), up, down, outw)


def solution(mesh):
    in_specs = (
        P("tm", None, "lat", None),
        P("tm", None, "lat", None),
        P("tm"),
        P(), P(), P(), P(), P(), P(), P(),
    )
    out_specs = P("tm", None, "lat", None)
    return jax.shard_map(shards, mesh=mesh, in_specs=in_specs, out_specs=out_specs, check_vma=False)
```

time: 657 us -> 81.7 us (0.12)
  the two profiles are of different devices: /device:TPU:249 before, /device:TPU:27 now
where the time goes in v1:
time: 81.7 us; the launch traced here: 81.4 us
  Pallas kernels  72.9 us (89%)
  local copies, waits for them, and re-layouts  7.84 us (10%)
    pallas_call x1, Pallas kernels, shards(): pl.pallas_call(kernel, out_shape=jax.ShapeDtypeStruct((1, NCH, NROW, NLON...  72.9 us
    unnamed x8, local copies, waits for them, and re-layouts  5.43 us
    pallas_call x1, local copies, waits for them, and re-layouts, shards(): pl.pallas_call(kernel, out_shape=jax.ShapeDtypeStruct((1, NCH, NROW, NLON...  2.4 us

profile of v1, /device:TPU:27, one launch (start us, length us, event | category | flops | bytes accessed | tf_op | source)
XLA Modules:
  0.0 81.4 jit_solution(16510134604966008289)
XLA Ops:
  0.0 0.0 copy-start
  0.7 1.7 %copy.14.outw = bf16[512,83]{1,0:T(8,128)(2,1)} copy(bf16[512,83]{0,1:T(8,128)(2,1)} %param.19) | data formatting | bytes 169984 | tf_op args[9]
  2.4 1.7 %copy.13.dw = f32[512,25]{1,0:T(8,128)} copy(f32[512,25]{0,1:T(8,128)} %param.15) | data formatting | bytes 102400 | tf_op args[5]
  4.1 0.0 copy-done
  4.1 0.0 copy-start.1
  4.1 0.9 %copy.11.traj = f32[1,83,6,192]{3,2,1,0:T(8,128)} copy(f32[1,83,6,192]{3,0,2,1:T(1,128)S(1)} %copy-done) | data formatting | bytes 764928 | tf_op args[0]
  5.0 0.2 copy-done.1
  5.2 0.9 %copy.12.noise = f32[1,83,6,192]{3,2,1,0:T(8,128)} copy(f32[1,83,6,192]{3,0,2,1:T(1,128)S(1)} %copy-done.1) | data formatting | bytes 764928 | tf_op args[1]
  6.1 72.9 %shard_map.100 = f32[1,83,6,192]{3,2,1,0:T(8,128)} custom-call(f32[1,83,6,192]{3,2,1,0:T(8,128)} %copy.11.traj, f32[1,83,6,192]{3,2,1,0:T(8,128)} %copy.12.noise, s32[1]{0:T(128)S(6)} %copy.16.step, bf16[83,512]{1,0:T(8,128)(2,1)} %emb.1, f32[512,512]{1,0:T(8,128)} %timew.1, f32[512,25]{1,0:T(8,128)} %copy.13.dw, f32[1,512]{1,0:T(1,128)} %bitcast.1, ...), custom_call_target="tpu_custom_call" | custom-call | tf_op jit(solution)/shard_map/pallas_call | solution.py:313
  79.0 2.4 %copy.15 = f32[1,83,6,192]{3,0,2,1:T(1,128)} copy(f32[1,83,6,192]{3,2,1,0:T(8,128)} %shard_map.100) | data formatting | bytes 764928 | tf_op jit(solution)/shard_map/pallas_call | solution.py:313
Async XLA Ops:
  0.0 4.1 %copy-start = (f32[1,83,6,192]{3,0,2,1:T(1,128)S(1)}, f32[1,83,6,192]{3,0,2,1:T(1,128)}, u32[]{:S(2)}) copy-start(f32[1,83,6,192]{3,0,2,1:T(1,128)} %param.10) | copy-start | bytes 1147396
  4.1 1.2 %copy-start.1 = (f32[1,83,6,192]{3,0,2,1:T(1,128)S(1)}, f32[1,83,6,192]{3,0,2,1:T(1,128)}, u32[]{:S(2)}) copy-start(f32[1,83,6,192]{3,0,2,1:T(1,128)} %param.11) | copy-start | bytes 1147396

commit v2 on v1

--- a/solution.py
+++ b/solution.py
@@ -35,13 +35,28 @@
 
 
 def kernel(
-    traj, noise, step, emb, timew, dw, gain, up_h, down_h, outw, out,
-    up, down, act, wb, conv, vt, dt, nz, condb,
+    traj, noise, step, emb, timew_h, taps, gain, up_h, down_h, outw, out,
+    up, down, timew, tin, nin, tout, act, wb, conv, vt, dt, nz, condb,
     ob, inb, retb0, retb1, st, stf, halo, rsrc, rbuf,
-    wsem, osend, isem, rsend, stsem, hsend, hrecv, rootsend, rootrecv,
+    wsem, iosem, osend, isem, rsend, stsem, hsend, hrecv, rootsend, rootrecv,
 ):
     t, l = lax.axis_index("tm"), lax.axis_index("lat")
 
+    def traj_in(r):
+        return pltpu.make_async_copy(traj.at[:, r, 0, :], tin.at[r], iosem.at[0, r])
+
+    def noise_in(r):
+        return pltpu.make_async_copy(noise.at[:, r, 0, :], nin.at[r], iosem.at[1, r])
+
+    def state_out(r):
+        return pltpu.make_async_copy(tout.at[r], out.at[:, r, 0, :], iosem.at[2, r])
+
+    for r in range(NROW):
+        traj_in(r).start()
+    ctime = pltpu.make_async_copy(timew_h, timew, wsem.at[2])
+    ctime.start()
+    for r in range(NROW):
+        noise_in(r).start()
     cup = pltpu.make_async_copy(up_h, up, wsem.at[0])
     cdown = pltpu.make_async_copy(down_h, down, wsem.at[1])
     cup.start()
@@ -58,16 +73,16 @@
     for shift in (1, 3):
         pl.semaphore_signal(barrier, inc=1, device_id={"lat": lax.rem(l + shift, 4)}, device_id_type=MESH)
 
+    for r in range(NROW):
+        traj_in(r).wait()
     pad = jnp.zeros((96 - NCH, 384), F32)
     for b in range(CHUNKS):
-        pair = jnp.concatenate([traj[0, :, 2 * b, :], traj[0, :, 2 * b + 1, :]], axis=1)
+        pair = jnp.concatenate([tin[2 * b], tin[2 * b + 1]], axis=1)
         dt[0:NCH, :] = pair
         dt[NCH:96, :] = pad
         whole = dt[0:96, :]
         to_tiles(rsrc.at[b], (), whole)
         to_tiles(st, (0, b), whole.astype(BF))
-        nz[b, 0:NCH, :] = jnp.concatenate([noise[0, :, 2 * b, :], noise[0, :, 2 * b + 1, :]], axis=1)
-        nz[b, NCH:96, :] = pad
 
     stepf = jnp.full((8, 512), step[0].astype(F32), F32)
     level = 2.0 * jnp.exp(stepf * (math.log(0.1) / (LEVELS - 1)))
@@ -76,16 +91,14 @@
     frequency = jnp.exp(jj * (-math.log(100.0) / 256))
     angles = jnp.log(level) * frequency
     features = jnp.where(j < 256, jnp.cos(angles), jnp.sin(angles))
+    ctime.wait()
     cond = jnp.dot(features, timew[...], precision=lax.Precision.HIGHEST, preferred_element_type=F32)
     condb[...] = cond * (1.0 / (1.0 + jnp.exp(-cond)))
     drift_scale = 0.125 * level[0:1, 0:384]
     noise_scale = 0.125 * jnp.sqrt(level[0:1, 0:384])
 
-    taps = jnp.transpose(dw[...])
     for k in range(25):
         wb[k] = jnp.broadcast_to(taps[k : k + 1, :], (8, D))
-
-    pl.semaphore_wait(barrier, NT + 1)
 
     def halo_up(it):
         return pltpu.make_async_remote_copy(
@@ -107,23 +120,25 @@
         def _():
             halo_down(it).start()
 
-    start_up(0)
-    start_down(0)
-
     def root_copy(k):
         return pltpu.make_async_remote_copy(
             src_ref=rsrc.at[k % 3, k // 3], dst_ref=rbuf, send_sem=rootsend, recv_sem=rootrecv,
             device_id={"tm": k}, device_id_type=MESH)
 
-    @pl.when(t == 0)
-    def _():
-        pltpu.make_async_copy(rsrc.at[0, 0], rbuf, rootrecv).start()
-
-        def one(k, _):
-            root_copy(k).start()
-            return 0
-
-        lax.fori_loop(1, OWNERS, one, 0)
+    def meet():
+        pl.semaphore_wait(barrier, NT + 1)
+        start_up(0)
+        start_down(0)
+
+        @pl.when(t == 0)
+        def _():
+            pltpu.make_async_copy(rsrc.at[0, 0], rbuf, rootrecv).start()
+
+            def one(k, _):
+                root_copy(k).start()
+                return 0
+
+            lax.fori_loop(1, OWNERS, one, 0)
 
     def embed(read, row0):
         vt[:, 0:96] = jnp.transpose(read)
@@ -145,26 +160,27 @@
     def convolve(b):
         for g in range(4):
             lanes = slice(g * 128, g * 128 + 128)
+            weight = [wb[k, :, lanes] for k in range(25)]
 
             def block(cb, _):
-                c0 = cb * 4
-                acc = [[None] * 4 for _ in range(2)]
+                c0 = cb * 2
+                acc = [[None] * 2 for _ in range(2)]
                 for ri in range(6):
-                    xs = [act[2 * b + ri, c0 + ci, :, lanes] for ci in range(8)]
+                    xs = [act[2 * b + ri, c0 + ci, :, lanes] for ci in range(6)]
                     for rr in range(2):
                         tap = ri - rr
                         if not 0 <= tap < 5:
                             continue
-                        for cc in range(4):
+                        for cc in range(2):
                             for tj in range(5):
-                                term = wb[tap * 5 + tj, :, lanes] * xs[cc + tj]
+                                term = weight[tap * 5 + tj] * xs[cc + tj]
                                 acc[rr][cc] = term if acc[rr][cc] is None else acc[rr][cc] + term
                 for rr in range(2):
-                    for cc in range(4):
+                    for cc in range(2):
                         conv[rr, c0 + cc, :, lanes] = acc[rr][cc]
                 return 0
 
-            lax.fori_loop(0, 6, block, 0)
+            lax.fori_loop(0, COL // 2, block, 0)
 
     def mlp(b):
         for rr in range(2):
@@ -178,7 +194,7 @@
             hidden = (0.5 * h * (1.0 + jnp.tanh(inner))).astype(BF)
             y = jnp.dot(hidden, down[...], preferred_element_type=F32)
             y = (act[2 + 2 * b + rr, 2 : 2 + COL].reshape(NLON, D) + y).astype(BF)
-            drift = jnp.dot(y, outw[...], preferred_element_type=F32)
+            drift = lax.dot_general(y, outw[...], (((1,), (1,)), ((), ())), preferred_element_type=F32)
             for c in range(COL):
                 vt[pl.ds(rr * NLON + c, SEG, stride=COL), 0:NCH] = drift[c * SEG : c * SEG + SEG, :]
         dT = jnp.transpose(vt[...])[0:96, :]
@@ -235,8 +251,6 @@
         dst = (st.at[1], stf)[it]
         pltpu.make_async_copy(dst.at[b], dst.at[b], stsem.at[it, b]).wait()
 
-    cup.wait()
-    cdown.wait()
     vt[...] = jnp.zeros(vt.shape, F32)
     for it in range(ITERS):
         if it == 1:
@@ -269,6 +283,15 @@
                 def _():
                     zero_rows(8)
             convolve(b)
+            if it == 0 and b == 1:
+                meet()
+                for r in range(NROW):
+                    noise_in(r).wait()
+                for bb in range(CHUNKS):
+                    nz[bb, 0:NCH, :] = jnp.concatenate([nin[2 * bb], nin[2 * bb + 1]], axis=1)
+                    nz[bb, NCH:96, :] = pad
+                cup.wait()
+                cdown.wait()
             to_tiles(ob, (it, b), mlp(b).astype(BF))
             send_chunk(it, b)
         scan(it)
@@ -276,8 +299,9 @@
     for b in (1, 0, 2):
         wait_chunk(1, b)
         value = from_tiles(stf, (b,))[0:NCH, :]
-        out[0, :, 2 * b, :] = value[:, 0:NLON]
-        out[0, :, 2 * b + 1, :] = value[:, NLON : 2 * NLON]
+        for rr in range(2):
+            tout[2 * b + rr] = value[:, rr * NLON : rr * NLON + NLON]
+            state_out(2 * b + rr).start()
 
     def drain(ref, sem):
         pltpu.make_async_copy(ref, ref, sem).wait()
@@ -288,6 +312,9 @@
         drain(rsrc.at[1], rootsend)
         drain(rsrc.at[2, pl.ds(0, TILES - 1)], rootsend)
 
+    for r in range(NROW):
+        state_out(r).wait()
+
     for it in range(ITERS):
         for b in range(CHUNKS):
             own = jnp.logical_and(mine_b == b, t < OWNERS)
@@ -310,14 +337,18 @@
     vm = pl.BlockSpec(memory_space=pltpu.VMEM)
     anyspace = pl.BlockSpec(memory_space=pl.ANY)
     dma = pltpu.SemaphoreType.DMA
-    return pl.pallas_call(
+    result = pl.pallas_call(
         kernel,
-        out_shape=jax.ShapeDtypeStruct((1, NCH, NROW, NLON), F32),
-        in_specs=[vm, vm, pl.BlockSpec(memory_space=pltpu.SMEM), vm, vm, vm, vm, anyspace, anyspace, vm],
-        out_specs=vm,
+        out_shape=jax.ShapeDtypeStruct((NCH, NROW, 1, NLON), F32),
+        in_specs=[anyspace, anyspace, pl.BlockSpec(memory_space=pltpu.SMEM), vm, anyspace, vm, vm, anyspace, anyspace, vm],
+        out_specs=anyspace,
         scratch_shapes=[
             pltpu.VMEM((D, FF), BF),
             pltpu.VMEM((FF, D), BF),
+            pltpu.VMEM((D, D), F32),
+            pltpu.VMEM((NROW, NCH, NLON), F32),
+            pltpu.VMEM((NROW, NCH, NLON), F32),
+            pltpu.VMEM((NROW, NCH, NLON), F32),
             pltpu.VMEM((10, COL + 4, SEG, D), F32),
             pltpu.VMEM((25, 8, D), F32),
             pltpu.VMEM((2, COL, SEG, D), F32),
@@ -334,7 +365,8 @@
             pltpu.VMEM((ITERS, 2, TILES, 16, 128), BF),
             pltpu.VMEM((CHUNKS, TILES, 16, 128), F32),
             pltpu.VMEM((16, 128), F32),
-            dma((2,)),
+            dma((3,)),
+            dma((3, NROW)),
             dma((ITERS, CHUNKS)),
             dma((ITERS,)),
             dma((ITERS,)),
@@ -347,7 +379,11 @@
         compiler_params=pltpu.CompilerParams(
             collective_id=0, has_side_effects=True, vmem_limit_bytes=56 * 2**20
         ),
-    )(traj, noise, step_index, emb, timew, dw, gain.reshape(1, D), up, down, outw)
+    )(
+        traj.reshape(NCH, NROW, 1, NLON), noise.reshape(NCH, NROW, 1, NLON), step_index,
+        emb, timew, dw.T, gain.reshape(1, D), up, down, outw.T,
+    )
+    return result.reshape(1, NCH, NROW, NLON)
 
 
 def solution(mesh):

time: 81.7 us -> 67.2 us (0.82)
  Pallas kernels: 72.9 us -> 64.2 us
  local copies, waits for them, and re-layouts: 7.84 us -> 2.17 us
    pallas_call x1, Pallas kernels: 72.9 us -> 64.2 us  [shards(): pl.pallas_call(kernel, out_shape=jax.ShapeDtypeStruct((NCH, NROW, 1, NLON...]
    unnamed x8 -> x1, local copies, waits for them, and re-layouts: 5.43 us -> 2.17 us
    pallas_call x1 -> x0, local copies, waits for them, and re-layouts: 2.4 us -> none  [shards(): pl.pallas_call(kernel, out_shape=jax.ShapeDtypeStruct((1, NCH, NROW, NLON...]
where the time goes in v2:
time: 67.2 us; the launch traced here: 67 us
  Pallas kernels  64.2 us (96%)
  local copies, waits for them, and re-layouts  2.17 us (3%)
    pallas_call x1, Pallas kernels, shards(): pl.pallas_call(kernel, out_shape=jax.ShapeDtypeStruct((NCH, NROW, 1, NLON...  64.2 us
    unnamed x1, local copies, waits for them, and re-layouts  2.17 us

profile of v2, /device:TPU:27, one launch (start us, length us, event | category | flops | bytes accessed | tf_op | source)
XLA Modules:
  0.0 67.0 jit_solution(9930790761287149110)
XLA Ops:
  0.7 64.2 %shard_map.100 = f32[83,6,1,192]{3,2,1,0:T(1,128)} custom-call(f32[83,6,1,192]{3,2,1,0:T(1,128)} %bitcast.7, f32[83,6,1,192]{3,2,1,0:T(1,128)} %bitcast.8, s32[1]{0:T(128)S(6)} %copy.12.step, bf16[83,512]{1,0:T(8,128)(2,1)} %emb.1, f32[512,512]{1,0:T(8,128)} %timew_h.1, f32[25,512]{1,0:T(8,128)} %bitcast.10, f32[1,512]{1,0:T(1,128)} %bitcast.11, ...), custom_call_target="tpu_custom_call" | custom-call | tf_op jit(solution)/shard_map/pallas_call | solution.py:340
  64.9 2.2 %copy.13 = f32[1,83,6,192]{3,0,2,1:T(1,128)} copy(f32[1,83,6,192]{3,0,2,1:T(1,128)} %bitcast.6) | data formatting | bytes 764928

commit v3 on v2

--- a/solution.py
+++ b/solution.py
@@ -17,7 +17,7 @@
 NT = 64
 CHUNKS, TILES = 3, 18
 OWNERS = CHUNKS * TILES
-RET = (BF, F32)
+RET = (BF, BF)
 D, FF = 512, 1024
 
 
@@ -41,6 +41,30 @@
     wsem, iosem, osend, isem, rsend, stsem, hsend, hrecv, rootsend, rootrecv,
 ):
     t, l = lax.axis_index("tm"), lax.axis_index("lat")
+    y, z, core = t // 16, (t // 2) % 8, t % 2
+
+    def others(do):
+        def ring(i, _):
+            half = (i + 1) // 2
+            dz = jnp.where(i % 2 == 0, 4 + half, 4 - half)
+            zz = lax.rem(z + dz, 8) * 2
+            for dy in (2, 1, 3, 0):
+                yy = lax.rem(y + dy, 4) * 16 + zz
+                for dc in (0, 1):
+                    do(yy + lax.rem(core + dc, 2))
+            return 0
+
+        lax.fori_loop(0, 7, ring, 0)
+        for dy in (2, 1, 3, 0):
+            for dc in (1, 0):
+                if dy or dc:
+                    do(lax.rem(y + dy, 4) * 16 + z * 2 + lax.rem(core + dc, 2))
+
+    barrier = pltpu.get_barrier_semaphore()
+    for shift in (1, 3):
+        pl.semaphore_signal(barrier, inc=1, device_id={"lat": lax.rem(l + shift, 4)}, device_id_type=MESH)
+    others(lambda s: pl.semaphore_signal(barrier, inc=1, device_id={"tm": s}, device_id_type=MESH))
+
 
     def traj_in(r):
         return pltpu.make_async_copy(traj.at[:, r, 0, :], tin.at[r], iosem.at[0, r])
@@ -61,17 +85,6 @@
     cdown = pltpu.make_async_copy(down_h, down, wsem.at[1])
     cup.start()
     cdown.start()
-
-    barrier = pltpu.get_barrier_semaphore()
-
-    def greet(k, _):
-        pl.semaphore_signal(barrier, inc=1, device_id={"tm": lax.rem(t + k, NT)}, device_id_type=MESH)
-        return 0
-
-    lax.fori_loop(1, NT, greet, 0)
-
-    for shift in (1, 3):
-        pl.semaphore_signal(barrier, inc=1, device_id={"lat": lax.rem(l + shift, 4)}, device_id_type=MESH)
 
     for r in range(NROW):
         traj_in(r).wait()
@@ -183,20 +196,22 @@
             lax.fori_loop(0, COL // 2, block, 0)
 
     def mlp(b):
+        x = conv[...].reshape(2 * NLON, D)
+        mean = jnp.mean(x, axis=1, keepdims=True)
+        x = x - mean
+        var = jnp.mean(x * x, axis=1, keepdims=True)
+        normed = (x * lax.rsqrt(var + 1e-6) * gain[...]).astype(BF)
+        h = jnp.dot(normed, up[...], preferred_element_type=F32)
+        half = 0.5 * h
+        inner = h * (0.7978845608028654 + (0.7978845608028654 * 0.044715) * (h * h))
+        hidden = (half + half * jnp.tanh(inner)).astype(BF)
+        y = jnp.dot(hidden, down[...], preferred_element_type=F32)
+        y = (act[2 + 2 * b : 4 + 2 * b, 2 : 2 + COL].reshape(2 * NLON, D) + y).astype(BF)
+        drift = lax.dot_general(y, outw[...], (((1,), (1,)), ((), ())), preferred_element_type=F32)
         for rr in range(2):
-            x = conv[rr].reshape(NLON, D)
-            mean = jnp.mean(x, axis=1, keepdims=True)
-            x = x - mean
-            var = jnp.mean(x * x, axis=1, keepdims=True)
-            normed = (x * lax.rsqrt(var + 1e-6) * gain[...]).astype(BF)
-            h = jnp.dot(normed, up[...], preferred_element_type=F32)
-            inner = 0.7978845608028654 * (h + 0.044715 * (h * h * h))
-            hidden = (0.5 * h * (1.0 + jnp.tanh(inner))).astype(BF)
-            y = jnp.dot(hidden, down[...], preferred_element_type=F32)
-            y = (act[2 + 2 * b + rr, 2 : 2 + COL].reshape(NLON, D) + y).astype(BF)
-            drift = lax.dot_general(y, outw[...], (((1,), (1,)), ((), ())), preferred_element_type=F32)
             for c in range(COL):
-                vt[pl.ds(rr * NLON + c, SEG, stride=COL), 0:NCH] = drift[c * SEG : c * SEG + SEG, :]
+                first = (rr * COL + c) * SEG
+                vt[pl.ds(rr * NLON + c, SEG, stride=COL), 0:NCH] = drift[first : first + SEG, :]
         dT = jnp.transpose(vt[...])[0:96, :]
         return drift_scale * dT + noise_scale * nz[b]
 
@@ -232,20 +247,17 @@
 
             def one(s, acc):
                 retb[s] = acc.astype(retb.dtype)
-
-                @pl.when(s == t)
-                def _():
-                    pltpu.make_async_copy(retb.at[s], dst.at[mine_b, mine_k], stsem.at[it, mine_b]).start()
-
-                @pl.when(s != t)
-                def _():
-                    pltpu.make_async_remote_copy(
-                        src_ref=retb.at[s], dst_ref=dst.at[mine_b, mine_k], send_sem=rsend.at[it],
-                        recv_sem=stsem.at[it, mine_b], device_id={"tm": s}, device_id_type=MESH).start()
-
                 return acc + inb[it, s].astype(F32)
 
-            lax.fori_loop(0, NT, one, rbuf[...])
+            lax.fori_loop(0, NT, one, rbuf[...], unroll=8)
+
+            def send(s):
+                pltpu.make_async_remote_copy(
+                    src_ref=retb.at[s], dst_ref=dst.at[mine_b, mine_k], send_sem=rsend.at[it],
+                    recv_sem=stsem.at[it, mine_b], device_id={"tm": s}, device_id_type=MESH).start()
+
+            others(send)
+            pltpu.make_async_copy(retb.at[t], dst.at[mine_b, mine_k], stsem.at[it, mine_b]).start()
 
     def wait_chunk(it, b):
         dst = (st.at[1], stf)[it]
@@ -253,13 +265,13 @@
 
     vt[...] = jnp.zeros(vt.shape, F32)
     for it in range(ITERS):
-        if it == 1:
-            wait_chunk(0, 0)
-            start_up(1)
-            wait_chunk(0, 2)
-            start_down(1)
-            wait_chunk(0, 1)
-        for b in range(CHUNKS):
+        for b in (1, 0, 2):
+            if it == 1:
+                wait_chunk(0, b)
+                if b == 0:
+                    start_up(1)
+                if b == 2:
+                    start_down(1)
             embed(from_tiles(st, (it, b)), 2 + 2 * b)
         for b in (1, 0, 2):
             if b == 0:

time: 67.2 us -> 65.3 us (0.972)
  the two profiles are of different devices: /device:TPU:27 before, /device:TPU:3 now
where the time goes in v3:
time: 65.3 us; the launch traced here: 65.1 us
  Pallas kernels  62.3 us (95%)
  local copies, waits for them, and re-layouts  2.17 us (3%)
  between operations  0.66 us (1%)
    pallas_call x1, Pallas kernels, shards(): pl.pallas_call(kernel, out_shape=jax.ShapeDtypeStruct((NCH, NROW, 1, NLON...  62.3 us
    unnamed x1, local copies, waits for them, and re-layouts  2.17 us

profile of v3, /device:TPU:3, one launch (start us, length us, event | category | flops | bytes accessed | tf_op | source)
XLA Modules:
  0.0 65.1 jit_solution(5110033756147397157)
XLA Ops:
  0.7 62.3 %shard_map.100 = f32[83,6,1,192]{3,2,1,0:T(1,128)} custom-call(f32[83,6,1,192]{3,2,1,0:T(1,128)} %bitcast.7, f32[83,6,1,192]{3,2,1,0:T(1,128)} %bitcast.8, s32[1]{0:T(128)S(6)} %copy.12.step, bf16[83,512]{1,0:T(8,128)(2,1)} %emb.1, f32[512,512]{1,0:T(8,128)} %timew_h.1, f32[25,512]{1,0:T(8,128)} %bitcast.10, f32[1,512]{1,0:T(1,128)} %bitcast.11, ...), custom_call_target="tpu_custom_call" | custom-call | tf_op jit(solution)/shard_map/pallas_call | solution.py:352
  63.0 2.2 %copy.13 = f32[1,83,6,192]{3,0,2,1:T(1,128)} copy(f32[1,83,6,192]{3,0,2,1:T(1,128)} %bitcast.6) | data formatting | bytes 764928

commit v4 on v3

--- a/solution.py
+++ b/solution.py
@@ -216,7 +216,8 @@
         return drift_scale * dT + noise_scale * nz[b]
 
     def send_chunk(it, b):
-        def one(k, _):
+        def one(i, _):
+            k = lax.rem(i + t, TILES)
             owner = 3 * k + b
 
             @pl.when(owner == t)

time: 65.3 us -> 64.7 us (level)
  the two profiles are of different devices: /device:TPU:3 before, /device:TPU:27 now
where the time goes in v4:
time: 64.7 us; the launch traced here: 63.7 us
  Pallas kernels  60.9 us (94%)
  local copies, waits for them, and re-layouts  2.17 us (3%)
  between operations  0.66 us (1%)
    pallas_call x1, Pallas kernels, shards(): pl.pallas_call(kernel, out_shape=jax.ShapeDtypeStruct((NCH, NROW, 1, NLON...  60.9 us
    unnamed x1, local copies, waits for them, and re-layouts  2.17 us

profile of v4, /device:TPU:27, one launch (start us, length us, event | category | flops | bytes accessed | tf_op | source)
XLA Modules:
  0.0 63.7 jit_solution(12598996229313603573)
XLA Ops:
  0.7 60.9 %shard_map.100 = f32[83,6,1,192]{3,2,1,0:T(1,128)} custom-call(f32[83,6,1,192]{3,2,1,0:T(1,128)} %bitcast.7, f32[83,6,1,192]{3,2,1,0:T(1,128)} %bitcast.8, s32[1]{0:T(128)S(6)} %copy.12.step, bf16[83,512]{1,0:T(8,128)(2,1)} %emb.1, f32[512,512]{1,0:T(8,128)} %timew_h.1, f32[25,512]{1,0:T(8,128)} %bitcast.10, f32[1,512]{1,0:T(1,128)} %bitcast.11, ...), custom_call_target="tpu_custom_call" | custom-call | tf_op jit(solution)/shard_map/pallas_call | solution.py:353
  61.5 2.2 %copy.13 = f32[1,83,6,192]{3,0,2,1:T(1,128)} copy(f32[1,83,6,192]{3,0,2,1:T(1,128)} %bitcast.6) | data formatting | bytes 764928
